TPU v7x, 32 devices: a whole 2x2x4 slice. The times are simulated.
32 devices in a mesh: dp: 8 (over z, y), tensor: 4 (over x, core).
Axes of the slice: x: 2, y: 2, z: 4, core: 2. Of those that a mesh axis runs over, the one named last changes fastest.
Arguments:
- tokens: bfloat16 [8192, 2048], P(('dp', 'tensor')), may hold values from -6 to 6
- ln_gain: float32 [2048], replicated, may hold values from 0.1 to 1.9
- ln_bias: float32 [2048], replicated, may hold values from -1.75 to 1.75
- w_qkv: bfloat16 [2048, 3, 2048], P('dp', None, 'tensor'), may hold values from -0.125 to 0.125
- b_qkv: float32 [3, 2048], P(None, 'tensor'), may hold values from -3 to 3
- w_out: bfloat16 [2048, 2048], P('tensor', 'dp'), may hold values from -0.5 to 0.5
- w_up: bfloat16 [2048, 8192], P('dp', 'tensor'), may hold values from -0.125 to 0.125
- b_up: float32 [8192], P('tensor'), may hold values from -3 to 3
- w_down: bfloat16 [8192, 2048], P('tensor', 'dp'), may hold values from -0.0625 to 0.0625
- out_bias: float32 [2048], replicated, may hold values from -3 to 3
- cotangent: bfloat16 [8192, 2048], P(('dp', 'tensor')), may hold values from -12 to 12, as said below
Outputs:
- output: bfloat16 [8192, 2048], P(('dp', 'tensor'))
- grad_tokens: float32 [8192, 2048], P(('dp', 'tensor'))
- grad_ln_gain: float32 [2048], replicated
- grad_ln_bias: float32 [2048], replicated
- grad_w_qkv: float32 [2048, 3, 2048], P('dp', None, 'tensor')
- grad_b_qkv: float32 [3, 2048], P(None, 'tensor')
- grad_w_out: float32 [2048, 2048], P('tensor', 'dp')
- grad_w_up: float32 [2048, 8192], P('dp', 'tensor')
- grad_b_up: float32 [8192], P('tensor')
- grad_w_down: float32 [8192, 2048], P('tensor', 'dp')
- grad_out_bias: float32 [2048], replicated
Inputs may be any that keep to these rules, and one draw needn't show every extreme that they name: cotangent of the block's output.
All inputs are finite; a program needn't handle non-finite values.
Results may differ from a plain program's by a relative error of at most 0.012.
The roundings to bfloat16 on the way count: a program that leaves them out, or rounds other values in their place, can miss the bound.
Values may be sent and summed in bfloat16 or wider, within the bound.
A program may use at most 256 MiB of HBM per device.

v0:
```python
import jax
import jax.numpy as jnp
from jax import lax
from jax.sharding import PartitionSpec as P

HEAD_DIM = 64
ROT = 32


epsilon = 1e-05
big_negative = -1e30


def rotary_tables(row_count):
    half_rot = ROT // 2
    positions = jnp.arange(row_count).astype(jnp.float32)
    freqs = 10000.0 ** (-(2.0 * jnp.arange(half_rot).astype(jnp.float32)) / ROT)
    angles = positions[:, None] * freqs[None, :]
    return (jnp.cos(angles)[:, None, :], jnp.sin(angles)[:, None, :])


def rotate(field, cosines, sines):
    half_rot = ROT // 2
    first = field[..., :half_rot]
    second = field[..., half_rot:ROT]
    return jnp.concatenate(
        [first * cosines - second * sines, second * cosines + first * sines, field[..., ROT:]],
        axis=-1,
    )


def gelu_tanh(values):
    return jax.nn.gelu(values, approximate=True)


def causal_scores(query_block, key_rows, block_index):
    block_len = query_block.shape[0]
    query_pos = block_index * block_len + jnp.arange(block_len)
    key_pos = jnp.arange(key_rows.shape[0])
    raw = jnp.einsum("qhd,khd->hqk", query_block, key_rows, preferred_element_type=jnp.float32)
    scaled = raw * HEAD_DIM ** (-0.5)
    return jnp.where(key_pos[None, None, :] <= query_pos[None, :, None], scaled, big_negative)


def attend_forward(queries, key_rows, value_rows, block_len):
    row_count, heads_here, head_size = queries.shape
    n_blocks = row_count // block_len
    query_blocks = queries.reshape(n_blocks, block_len, heads_here, head_size)

    def one_block(item):
        query_block, block_index = item
        scores = causal_scores(query_block, key_rows, block_index)
        top_score = jnp.max(scores, axis=2, keepdims=True)
        exponent = jnp.exp(scores - top_score)
        totals = jnp.sum(exponent, axis=2, keepdims=True)
        probability = (exponent / totals).astype(jnp.bfloat16)
        attended = jnp.einsum(
            "hqk,khd->qhd", probability, value_rows, preferred_element_type=jnp.float32
        )
        return (attended, (top_score + jnp.log(totals))[:, :, 0])

    attended, logsum = lax.map(one_block, (query_blocks, jnp.arange(n_blocks)))
    return (attended.reshape(row_count, heads_here * head_size), logsum)


def attend_backward(queries, key_rows, value_rows, grad_att, logsum, block_len):
    row_count, heads_here, head_size = queries.shape
    n_blocks = row_count // block_len
    query_blocks = queries.reshape(n_blocks, block_len, heads_here, head_size)
    grad_blocks = grad_att.reshape(n_blocks, block_len, heads_here, head_size)
    scaling = HEAD_DIM ** (-0.5)

    def one_block(carry, item):
        grad_keys, grad_values = carry
        query_block, grad_block, lse_block, block_index = item
        scores = causal_scores(query_block, key_rows, block_index)
        probability = jnp.exp(scores - lse_block[:, :, None])
        grad_probs = jnp.einsum(
            "qhd,khd->hqk", grad_block, value_rows, preferred_element_type=jnp.float32
        )
        centre = jnp.sum(grad_probs * probability, axis=2, keepdims=True)
        grad_scores = (probability * (grad_probs - centre) * scaling).astype(jnp.bfloat16)
        grad_query = jnp.einsum(
            "hqk,khd->qhd", grad_scores, key_rows, preferred_element_type=jnp.float32
        )
        grad_keys = grad_keys + jnp.einsum(
            "hqk,qhd->khd", grad_scores, query_block, preferred_element_type=jnp.float32
        )
        grad_values = grad_values + jnp.einsum(
            "hqk,qhd->khd",
            probability.astype(jnp.bfloat16),
            grad_block,
            preferred_element_type=jnp.float32,
        )
        return ((grad_keys, grad_values), grad_query)

    zero_rows = jnp.zeros(key_rows.shape, jnp.float32)
    (grad_keys, grad_values), grad_queries = lax.scan(
        one_block, (zero_rows, zero_rows), (query_blocks, grad_blocks, logsum, jnp.arange(n_blocks))
    )
    return (grad_queries.reshape(row_count, heads_here, head_size), grad_keys, grad_values)


def shards(tokens, ln_gain, ln_bias, w_qkv, b_qkv, w_out, w_up, b_up, w_down, out_bias, cotangent):
    activ = tokens.astype(jnp.float32)
    average = jnp.mean(activ, axis=1, keepdims=True)
    centered = activ - average
    variance = jnp.mean(centered * centered, axis=1, keepdims=True)
    inv_std = lax.rsqrt(variance + epsilon)
    x_hat = centered * inv_std
    normed = lax.all_gather(
        (x_hat * ln_gain + ln_bias).astype(jnp.bfloat16), "tensor", axis=0, tiled=True
    )
    row_count = normed.shape[0]
    block_len = min(row_count, 512)
    qkv_full, out_full, up_full, down_full = (
        lax.all_gather(w_qkv, "dp", axis=0, tiled=True),
        lax.all_gather(w_out, "dp", axis=1, tiled=True),
        lax.all_gather(w_up, "dp", axis=0, tiled=True),
        lax.all_gather(w_down, "dp", axis=1, tiled=True),
    )
    heads_here = w_qkv.shape[2] // HEAD_DIM
    local_width = heads_here * HEAD_DIM
    head_shape = (row_count, heads_here, HEAD_DIM)
    project = (
        jnp.einsum("td,dcf->tcf", normed, qkv_full, preferred_element_type=jnp.float32) + b_qkv
    )
    cosines, sines = rotary_tables(row_count)
    queries = rotate(project[:, 0].reshape(head_shape), cosines, sines).astype(jnp.bfloat16)
    key_rows = rotate(project[:, 1].reshape(head_shape), cosines, sines).astype(jnp.bfloat16)
    value_rows = project[:, 2].reshape(head_shape).astype(jnp.bfloat16)
    attended, logsum = attend_forward(queries, key_rows, value_rows, block_len)
    attended = attended.astype(jnp.bfloat16)
    hidden = jnp.dot(normed, up_full, preferred_element_type=jnp.float32) + b_up
    activated = gelu_tanh(hidden).astype(jnp.bfloat16)
    partial_rows = jnp.dot(attended, out_full, preferred_element_type=jnp.float32) + jnp.dot(
        activated, down_full, preferred_element_type=jnp.float32
    )
    summed = lax.psum_scatter(partial_rows, "tensor", scatter_dimension=0, tiled=True)
    output = (activ + summed + out_bias).astype(jnp.bfloat16)
    grad_local = cotangent.astype(jnp.float32)
    grad_rows = lax.all_gather(cotangent, "tensor", axis=0, tiled=True)
    grad_down = jnp.einsum("tf,td->fd", activated, grad_rows, preferred_element_type=jnp.float32)
    grad_act = jnp.einsum("td,fd->tf", grad_rows, down_full, preferred_element_type=jnp.float32)
    gelu_pull = jax.vjp(gelu_tanh, hidden)[1]
    grad_hidden = gelu_pull(grad_act)[0].astype(jnp.bfloat16)
    grad_up = jnp.einsum("td,tf->df", normed, grad_hidden, preferred_element_type=jnp.float32)
    grad_b_up = jnp.sum(grad_hidden.astype(jnp.float32), axis=0)
    grad_normed = jnp.einsum("tf,df->td", grad_hidden, up_full, preferred_element_type=jnp.float32)
    grad_out = jnp.einsum("tf,td->fd", attended, grad_rows, preferred_element_type=jnp.float32)
    grad_att = jnp.einsum(
        "td,fd->tf", grad_rows, out_full, preferred_element_type=jnp.float32
    ).astype(jnp.bfloat16)
    grad_queries, grad_keys, grad_values = attend_backward(
        queries, key_rows, value_rows, grad_att.reshape(head_shape), logsum, block_len
    )
    grad_q_pre = rotate(grad_queries, cosines, -sines).reshape(row_count, local_width)
    grad_k_pre = rotate(grad_keys, cosines, -sines).reshape(row_count, local_width)
    grad_project = jnp.stack(
        [grad_q_pre, grad_k_pre, grad_values.reshape(row_count, local_width)], axis=1
    ).astype(jnp.bfloat16)
    grad_qkv = jnp.einsum("td,tcf->dcf", normed, grad_project, preferred_element_type=jnp.float32)
    grad_b_qkv = jnp.sum(grad_project.astype(jnp.float32), axis=0)
    grad_normed = grad_normed + jnp.einsum(
        "tcf,dcf->td", grad_project, qkv_full, preferred_element_type=jnp.float32
    )
    grad_ln_out = lax.psum_scatter(grad_normed, "tensor", scatter_dimension=0, tiled=True)
    qkv_summed, out_summed, up_summed, down_summed = (
        lax.psum_scatter(grad_qkv, "dp", scatter_dimension=0, tiled=True),
        lax.psum_scatter(grad_out, "dp", scatter_dimension=1, tiled=True),
        lax.psum_scatter(grad_up, "dp", scatter_dimension=0, tiled=True),
        lax.psum_scatter(grad_down, "dp", scatter_dimension=1, tiled=True),
    )
    scaled_grad = grad_ln_out * ln_gain
    grad_tokens = (
        inv_std
        * (
            scaled_grad
            - jnp.mean(scaled_grad, axis=1, keepdims=True)
            - x_hat * jnp.mean(scaled_grad * x_hat, axis=1, keepdims=True)
        )
        + grad_local
    )
    gain_grad, shift_grad, bias_grad = lax.psum(
        (
            jnp.sum(grad_ln_out * x_hat, axis=0),
            jnp.sum(grad_ln_out, axis=0),
            jnp.sum(grad_local, axis=0),
        ),
        ("dp", "tensor"),
    )
    qkv_bias_grad, up_bias_grad = lax.psum((grad_b_qkv, grad_b_up), "dp")
    return (
        output,
        grad_tokens,
        gain_grad,
        shift_grad,
        qkv_summed,
        qkv_bias_grad,
        out_summed,
        up_summed,
        up_bias_grad,
        down_summed,
        bias_grad,
    )


def solution(mesh):
    placed = (
        P(("dp", "tensor"), None),
        P(),
        P(),
        P("dp", None, "tensor"),
        P(None, "tensor"),
        P("tensor", "dp"),
        P("dp", "tensor"),
        P("tensor"),
        P("tensor", "dp"),
        P(),
        P(("dp", "tensor"), None),
    )
    return jax.shard_map(
        shards,
        mesh=mesh,
        in_specs=placed,
        out_specs=(
            P(("dp", "tensor"), None),
            P(("dp", "tensor"), None),
            P(),
            P(),
            P("dp", None, "tensor"),
            P(None, "tensor"),
            P("tensor", "dp"),
            P("dp", "tensor"),
            P("tensor"),
            P("tensor", "dp"),
            P(),
        ),
        check_vma=False,
    )
```

profile of v0, /device:TPU:27, one launch (start us, length us, event | category | flops | bytes accessed | tf_op | source)
XLA Modules:
  0.0 1579.6 jit_solution(5094459234250231309)
XLA Ops:
  12.4 2.7 fusion.69
  18.6 41.8 %all-gather.11.cloned.1.call-done = bf16[512,2048]{1,0:T(8,128)(2,1)} async-done(((bf16[512,256]{1,0:T(8,128)(2,1)}), bf16[512,2048]{1,0:T(8,128)(2,1)}) %all-gather.11.cloned.1.call-update) | async-done | bytes 2097168 | tf_op jit(solution)/shard_map/all_gather | solution.py:118
  60.4 35.5 %all-gather.17.cloned.1.call-done = bf16[1024,2048]{1,0:T(8,128)(2,1)} async-done(((bf16[256,2048]{1,0:T(8,128)(2,1)}), bf16[1024,2048]{1,0:T(8,128)(2,1)}) %all-gather.17.cloned.1.call-update) | async-done | bytes 4194320 | tf_op jit(solution)/shard_map/all_gather | solution.py:142
  95.9 5.2 convolution_convert_fusion
  104.7 27.9 %all-gather.7.cloned.1.call-done = bf16[1024,2048]{1,0:T(8,128)(2,1)} async-done(((bf16[256,2048]{1,0:T(8,128)(2,1)}), bf16[1024,2048]{1,0:T(8,128)(2,1)}) %all-gather.7.cloned.1.call-update) | async-done | bytes 4194320 | tf_op jit(solution)/shard_map/all_gather | solution.py:111
  132.5 101.2 %all-gather.9.cloned.1.call-done = bf16[2048,3,512]{0,2,1:T(8,128)(2,1)} async-done(((bf16[256,3,512]{0,2,1:T(8,128)(2,1)}), bf16[2048,3,512]{0,2,1:T(8,128)(2,1)}) %all-gather.9.cloned.1.call-update) | async-done | bytes 6291472 | tf_op jit(solution)/shard_map/all_gather | solution.py:117
  233.8 10.1 broadcast_add_fusion
  248.5 32.3 %while.27 = (s32[]{:T(128)}, bf16[2,512,8,64]{1,3,2,0:T(8,128)(2,1)S(1)}, f32[2,8,512]{2,1,0:T(8,128)S(1)}, s32[2]{0:T(128)S(1)}, bf16[2,512,8,64]{1,3,2,0:T(8,1...) while((s32[]{:T(128)}, ...), condition=%wide.region_5.6_spmd, body=%wide.region_2.5_spmd.sunk | while | flops 1124594176 | bytes 56234624 | solution.py:62
  250.1 4.9 fusion.128
  254.9 4.2 fusion.129
  259.2 5.4 fusion.130
  266.2 4.8 fusion.128
  271.1 4.2 fusion.129
  275.3 5.4 fusion.130
  281.7 193.8 %while.28 = (s32[]{:T(128)}, f32[1024,8,64]{0,2,1:T(8,128)}, f32[1024,8,64]{0,2,1:T(8,128)}, f32[2,512,8,64]{1,0,3,2:T(2,128)}, bf16[2,512,8,64]{1,3,2,0:T(8,128...) while((s32[]{:T(128)}, f32[1024,8,64]{0,2,1:T(8,128)}, ...), condition=%wide.region_9.10_spmd.clone, body=%wide.region_7.9_spmd.clone.sunk | while | flops 2745707008 | bytes 187750608 | solution.py:98
  283.7 9.8 subtract_exponential_fusion.3
  293.5 9.1 fusion.141
  302.7 22.0 %fusion.142 = f32[1,512,8,64]{1,3,2,0:T(8,128)S(1)} fusion(bf16[1024,8,64]{0,2,1:T(8,128)(2,1)} %get-tuple-element.397, f32[8,512,1024]{2,1,0:T(8,128)} %subtract_exponential_fusion.3, f32[8,512,1024]{2,1,0:T(8,128)} %fusion.141), kind=kOutput, calls=%fused_computation.31.clone.1 | convolution fusion | flops 557847552 | bytes 35651584 | tf_op jit(solution)/shard_map/while/body/eval_jaxpr/hqk,khd->qhd/dot_general | solution.py:83
  325.8 19.6 %dynamic_update_slice.19 = f32[2,512,8,64]{1,0,3,2:T(2,128)} dynamic-update-slice(f32[2,512,8,64]{1,0,3,2:T(2,128)} %get-tuple-element.381, f32[1,512,8,64]{1,0,3,2:T(1,128)S(1)} %copy.69, s32[]{:T(128)} %get-tuple-element.378, s32[]{:T(128)} %constant.33.clone.1..sunk, s32[]{:T(128)} %constant.33.clone.1..sunk, s32[]{:T(128)} %constant.33.clone.1..sunk) | dynamic-update-slice | bytes 2097156 | tf_op jit(solution)/shard_map/while/body/jit(dynamic_update_index_in_dim)/dynamic_update_slice | solution.py:62
  345.4 23.5 %bitcast_add_fusion.5 = f32[1024,8,64]{0,2,1:T(8,128)} fusion(f32[1024,8,64]{0,2,1:T(8,128)} %get-tuple-element.379, f32[8,512,1024]{2,1,0:T(8,128)} %subtract_exponential_fusion.3, f32[8,512,1024]{2,1,0:T(8,128)} %fusion.141, pred[]{:T(512)S(6)} %compare.3, bf16[2,512,8,64]{1,3,2,0:T(8,128)(2,1)} %get-tuple-element.395, s32[]{:T(128)} %get-tuple-element.378), kind=kOutput, calls=%fused_computation.29.clone.1 | convolution fusion | flops 558896128 | bytes 71827968 | tf_op jit(solution)/shard_map/while/body/eval_jaxpr/hqk,qhd->khd/dot_general | solution.py:86
  368.8 8.4 bitcast_add_fusion.6
  380.3 9.4 subtract_exponential_fusion.3
  389.7 9.1 fusion.141
  398.8 22.7 %fusion.142 = f32[1,512,8,64]{1,3,2,0:T(8,128)S(1)} fusion(bf16[1024,8,64]{0,2,1:T(8,128)(2,1)} %get-tuple-element.397, f32[8,512,1024]{2,1,0:T(8,128)} %subtract_exponential_fusion.3, f32[8,512,1024]{2,1,0:T(8,128)} %fusion.141), kind=kOutput, calls=%fused_computation.31.clone.1 | convolution fusion | flops 557847552 | bytes 35651584 | tf_op jit(solution)/shard_map/while/body/eval_jaxpr/hqk,khd->qhd/dot_general | solution.py:83
  422.6 19.6 %dynamic_update_slice.19 = f32[2,512,8,64]{1,0,3,2:T(2,128)} dynamic-update-slice(f32[2,512,8,64]{1,0,3,2:T(2,128)} %get-tuple-element.381, f32[1,512,8,64]{1,0,3,2:T(1,128)S(1)} %copy.69, s32[]{:T(128)} %get-tuple-element.378, s32[]{:T(128)} %constant.33.clone.1..sunk, s32[]{:T(128)} %constant.33.clone.1..sunk, s32[]{:T(128)} %constant.33.clone.1..sunk) | dynamic-update-slice | bytes 2097156 | tf_op jit(solution)/shard_map/while/body/jit(dynamic_update_index_in_dim)/dynamic_update_slice | solution.py:62
  442.2 24.2 %bitcast_add_fusion.5 = f32[1024,8,64]{0,2,1:T(8,128)} fusion(f32[1024,8,64]{0,2,1:T(8,128)} %get-tuple-element.379, f32[8,512,1024]{2,1,0:T(8,128)} %subtract_exponential_fusion.3, f32[8,512,1024]{2,1,0:T(8,128)} %fusion.141, pred[]{:T(512)S(6)} %compare.3, bf16[2,512,8,64]{1,3,2,0:T(8,128)(2,1)} %get-tuple-element.395, s32[]{:T(128)} %get-tuple-element.378), kind=kOutput, calls=%fused_computation.29.clone.1 | convolution fusion | flops 558896128 | bytes 71827968 | tf_op jit(solution)/shard_map/while/body/eval_jaxpr/hqk,qhd->khd/dot_general | solution.py:86
  466.4 7.8 bitcast_add_fusion.6
  475.5 3.1 reshape.228
  486.3 2.5 copy.41
  491.4 14.9 fusion.82
  506.3 18.9 %convert_reduce_fusion = (f32[2048]{0:T(1024)S(1)}, bf16[1024,2048]{1,0:T(8,128)(2,1)S(1)}) fusion(f32[1024,2048]{1,0:T(8,128)} %fusion.82, f32[2048]{0:T(1024)S(1)} %copy-done.24, bf16[1024,2048]{1,0:T(8,128)(2,1)} %all-gather.17.cloned.1.call-done, bf16[2048,2048]{1,0:T(8,128)(2,1)} %all-gather.15.cloned.1.call-done), kind=kOutput, calls=%fused_computation.61 | convolution fusion | flops 8638167040 | bytes 25182208 | tf_op jit(solution)/shard_map/td,fd->tf/dot_general | solution.py:144
  525.2 11.3 fusion.83
  536.5 12.8 bitcast_add_fusion.2
  551.8 16.8 %fusion.79 = f32[1024,2048]{1,0:T(8,128)S(1)} fusion(bf16[2048,2048]{1,0:T(8,128)(2,1)} %all-gather.15.cloned.1.call-done, f32[1024,2048]{1,0:T(8,128)} %fusion.82, f32[2048]{0:T(1024)S(1)} %copy-done.24), kind=kOutput, calls=%fused_computation.122 | convolution fusion | flops 8610906112 | bytes 25174016 | tf_op jit(solution)/shard_map/dot_general | solution.py:136
  568.6 5.9 convolution_add_fusion
  574.5 6.5 fusion.84
  581.1 12.3 fusion.56
  593.5 15.5 fusion.85
  609.0 17.2 %fusion.78 = f32[2048,2048]{1,0:T(8,128)} fusion(bf16[1024,2048]{1,0:T(8,128)(2,1)} %all-gather.17.cloned.1.call-done, f32[1024,2048]{1,0:T(8,128)} %fusion.82, f32[2048]{0:T(1024)S(1)} %copy-done.24), kind=kOutput, calls=%fused_computation.121 | convolution fusion | flops 8610906112 | bytes 29368320 | tf_op jit(solution)/shard_map/tf,td->fd/dot_general | solution.py:143
  628.4 26.5 %all-reduce.1 = (f32[3,512]{1,0:T(4,128)}, f32[2048]{0:T(1024)}) all-reduce(f32[3,512]{1,0:T(4,128)S(1)} %convert_reduce_fusion.1, f32[2048]{0:T(1024)S(1)} %get-tuple-element.204), channel_id=1, replica_groups=mesh['dp'=8,'tensor'=4] {'dp'}, use_global_device_ids=true, to_apply=%region_19.20 | all-reduce | flops 3584 | bytes 28672 | tf_op jit(solution)/shard_map/psum | solution.py:192
  655.0 2.7 fusion.73
  657.7 37.2 %reduce-scatter.7.cloned.1.call-done = f32[256,2048]{1,0:T(8,128)} async-done(((f32[1024,2048]{1,0:T(8,128)}), f32[256,2048]{1,0:T(8,128)}) %reduce-scatter.7.cloned.1.call-update) | async-done | bytes 2097168 | tf_op jit(solution)/shard_map/reduce_scatter | solution.py:139
  694.9 5.2 convert_reduce_fusion.3
  700.1 42.2 %all-reduce = (f32[2048]{0:T(1024)}, f32[2048]{0:T(1024)}, f32[2048]{0:T(1024)}) all-reduce(f32[2048]{0:T(1024)S(1)} %get-tuple-element.161, f32[2048]{0:T(1024)S(1)} %get-tuple-element.164, f32[2048]{0:T(1024)S(1)} %get-tuple-element.218), channel_id=1, replica_groups=mesh['dp'=8,'tensor'=4] {'dp','tensor'}, use_global_device_ids=true, to_apply=%region_14.15 | all-reduce | flops 6144 | bytes 49152 | tf_op jit(solution)/shard_map/psum | solution.py:184
  742.3 46.2 %reduce-scatter.13.cloned.1.call-done = f32[512,256]{1,0:T(8,128)} async-done(((f32[512,2048]{1,0:T(8,128)}), f32[512,256]{1,0:T(8,128)}) %reduce-scatter.13.cloned.1.call-update) | async-done | bytes 524304 | tf_op jit(solution)/shard_map/reduce_scatter | solution.py:170
  788.5 211.3 %reduce-scatter.11.cloned.1.call-done = f32[256,3,512]{2,0,1:T(8,128)} async-done(((f32[2048,3,512]{2,0,1:T(8,128)}), f32[256,3,512]{2,0,1:T(8,128)}) %reduce-scatter.11.cloned.1.call-update) | async-done | bytes 1572880 | tf_op jit(solution)/shard_map/reduce_scatter | solution.py:169
  999.8 286.8 %reduce-scatter.15.cloned.1.call-done = f32[256,2048]{1,0:T(8,128)} async-done(((f32[2048,2048]{1,0:T(8,128)}), f32[256,2048]{1,0:T(8,128)}) %reduce-scatter.15.cloned.1.call-update) | async-done | bytes 2097168 | tf_op jit(solution)/shard_map/reduce_scatter | solution.py:171
  1286.6 286.0 %reduce-scatter.17.cloned.1.call-done = f32[2048,256]{1,0:T(8,128)} async-done(((f32[2048,2048]{1,0:T(8,128)}), f32[2048,256]{1,0:T(8,128)}) %reduce-scatter.17.cloned.1.call-update) | async-done | bytes 2097168 | tf_op jit(solution)/shard_map/reduce_scatter | solution.py:172
  (139 shorter events, 41.4 us)
Async XLA Ops:
  7.2 8.0 copy-start.12
  7.2 53.2 %all-gather.11.cloned.1.call-start = ((), (), s32[]{:S(2)}) async-start(), calls=%async_computation.8 | async-start | bytes 2359296 | tf_op jit(solution)/shard_map/all_gather | solution.py:118
  7.9 88.0 %all-gather.17.cloned.1.call-start = ((), (), s32[]{:S(2)}) async-start(), calls=%async_computation.12 | async-start | bytes 5242880 | tf_op jit(solution)/shard_map/all_gather | solution.py:142
  8.7 123.9 %all-gather.7.cloned.1.call-start = ((), (), s32[]{:S(2)}) async-start(), calls=%async_computation.6 | async-start | bytes 5242880 | tf_op jit(solution)/shard_map/all_gather | solution.py:111
  10.2 1.7 copy-start.17
  11.8 0.6 copy-start.19
  15.1 218.7 %all-gather.9.cloned.1.call-start = ((), (), s32[]{:S(2)}) async-start(), calls=%async_computation.7 | async-start | bytes 7077888 | tf_op jit(solution)/shard_map/all_gather | solution.py:117
  16.3 475.1 %all-gather.13.cloned.1.call-start = ((), (), s32[]{:S(2)}) async-start(), calls=%async_computation.9 | async-start | bytes 9437184 | tf_op jit(solution)/shard_map/all_gather | solution.py:119
  16.9 489.4 %all-gather.15.cloned.1.call-start = ((), (), s32[]{:S(2)}) async-start(), calls=%async_computation.10 | async-start | bytes 9437184 | tf_op jit(solution)/shard_map/all_gather | solution.py:120
  17.5 637.4 %reduce-scatter.9.cloned.1.call-start = ((), (), s32[]{:S(2)}) async-start(), calls=%async_computation.13 | async-start | bytes 10485760 | tf_op jit(solution)/shard_map/reduce_scatter | solution.py:167
  18.6 226.2 %copy-start.13 = (f32[1024,16]{0,1:T(8,128)}, f32[1024,16]{0,1:T(8,128)S(1)}, u32[]{:S(2)}) copy-start(f32[1024,16]{0,1:T(8,128)S(1)} %get-tuple-element.227) | copy-start | bytes 196612
  101.1 132.7 %copy-start.23 = (f32[3,512]{1,0:T(4,128)S(1)}, f32[3,512]{1,0:T(4,128)}, u32[]{:S(2)}) copy-start(f32[3,512]{1,0:T(4,128)} %param.19) | copy-start | bytes 18436
  244.4 4.0 copy-start.9
  280.7 1.0 copy-start.10
  345.4 23.5 %copy-start = (f32[1024,8,64]{0,2,1:T(8,128)S(1)}, f32[1024,8,64]{0,2,1:T(8,128)}, u32[]{:S(2)}) copy-start(f32[1024,8,64]{0,2,1:T(8,128)} %get-tuple-element.380) | copy-start | bytes 6291460 | tf_op jit(solution)/shard_map/while
  377.3 1.3 copy-start.1
  442.2 24.2 %copy-start = (f32[1024,8,64]{0,2,1:T(8,128)S(1)}, f32[1024,8,64]{0,2,1:T(8,128)}, u32[]{:S(2)}) copy-start(f32[1024,8,64]{0,2,1:T(8,128)} %get-tuple-element.380) | copy-start | bytes 6291460 | tf_op jit(solution)/shard_map/while
  474.2 1.3 copy-start.1
  475.5 5.9 copy-start.14
  475.5 5.9 copy-start.15
  478.6 1.3 copy-start.4
  479.9 8.8 copy-start.2
  491.4 45.1 %copy-start.7 = (bf16[1024,1,512]{2,0,1:T(8,128)(2,1)}, bf16[1024,1,512]{2,0,1:T(8,128)(2,1)S(1)}, u32[]{:S(2)}) copy-start(bf16[1024,1,512]{2,0,1:T(8,128)(2,1)S(1)} %copy.42) | copy-start | bytes 3145732
  491.4 14.9 copy-start.24
  506.3 18.9 %copy-start.22 = (bf16[2048,2048]{1,0:T(8,128)(2,1)S(1)}, bf16[2048,2048]{1,0:T(8,128)(2,1)}, u32[]{:S(2)}) copy-start(bf16[2048,2048]{1,0:T(8,128)(2,1)} %all-gather.13.cloned.1.call-done) | copy-start | bytes 25165828
  525.2 11.3 copy-start.25
  525.2 11.3 copy-start.6
  549.3 1.2 copy-start.11
  549.3 145.6 %reduce-scatter.7.cloned.1.call-start = ((), (), s32[]{:S(2)}) async-start(), calls=%async_computation.11 | async-start | bytes 10485760 | tf_op jit(solution)/shard_map/reduce_scatter | solution.py:139
  551.8 16.8 %copy-start.8 = (bf16[512,2048]{1,0:T(8,128)(2,1)S(1)}, bf16[512,2048]{1,0:T(8,128)(2,1)}, u32[]{:S(2)}) copy-start(bf16[512,2048]{1,0:T(8,128)(2,1)} %all-gather.11.cloned.1.call-done) | copy-start | bytes 6291460
  574.5 214.0 %reduce-scatter.13.cloned.1.call-start = ((), (), s32[]{:S(2)}) async-start(), calls=%async_computation.15 | async-start | bytes 4718592 | tf_op jit(solution)/shard_map/reduce_scatter | solution.py:170
  581.0 418.8 %reduce-scatter.11.cloned.1.call-start = ((), (), s32[]{:S(2)}) async-start(), calls=%async_computation.14 | async-start | bytes 14155776 | tf_op jit(solution)/shard_map/reduce_scatter | solution.py:169
  593.4 693.2 %reduce-scatter.15.cloned.1.call-start = ((), (), s32[]{:S(2)}) async-start(), calls=%async_computation.16 | async-start | bytes 18874368 | tf_op jit(solution)/shard_map/reduce_scatter | solution.py:171
  609.0 963.6 %reduce-scatter.17.cloned.1.call-start = ((), (), s32[]{:S(2)}) async-start(), calls=%async_computation.17 | async-start | bytes 18874368 | tf_op jit(solution)/shard_map/reduce_scatter | solution.py:172
  626.2 28.8 %copy-start.3 = (bf16[256,2048]{1,0:T(8,128)(2,1)S(1)}, bf16[256,2048]{1,0:T(8,128)(2,1)}, u32[]{:S(2)}) copy-start(bf16[256,2048]{1,0:T(8,128)(2,1)} %param.15) | copy-start | bytes 3145732
  626.2 28.8 %copy-start.16 = (f32[2048]{0:T(1024)S(1)}, f32[2048]{0:T(1024)}, u32[]{:S(2)}) copy-start(f32[2048]{0:T(1024)} %param.16) | copy-start | bytes 24580
  626.2 28.8 %copy-start.18 = (f32[256]{0:T(256)S(1)}, f32[256]{0:T(256)}, u32[]{:S(2)}) copy-start(f32[256]{0:T(256)} %copy-done.17) | copy-start | bytes 3076
  626.2 28.8 %copy-start.20 = (f32[256]{0:T(256)S(1)}, f32[256]{0:T(256)}, u32[]{:S(2)}) copy-start(f32[256]{0:T(256)} %copy-done.19) | copy-start | bytes 3076
  626.2 68.7 %copy-start.5 = (bf16[256,2048]{1,0:T(8,128)(2,1)S(1)}, bf16[256,2048]{1,0:T(8,128)(2,1)}, u32[]{:S(2)}) copy-start(bf16[256,2048]{1,0:T(8,128)(2,1)} %param.25) | copy-start | bytes 3145732
  626.3 68.7 %copy-start.21 = (f32[2048]{0:T(1024)S(1)}, f32[2048]{0:T(1024)}, u32[]{:S(2)}) copy-start(f32[2048]{0:T(1024)} %param.24) | copy-start | bytes 24580
Sparse Core Ops, SparseCore 0:
  10.1 50.3 all-gather.10
  62.0 33.8 all-gather.16
  98.0 34.4 all-gather.6
  135.0 98.7 all-gather.8
  235.8 123.1 all-gather.12
  360.8 123.5 all-gather.14
  549.4 70.9 reduce-scatter.8
  623.2 71.6 reduce-scatter.6
  699.1 89.2 reduce-scatter.12
  792.9 206.8 reduce-scatter.10
  1004.6 281.9 reduce-scatter.14
  1290.8 281.6 reduce-scatter.16
where the time goes:
time: 1590 us; the launch traced here: 1580 us
  waiting for transfers between devices  1080 us (68%)
  matrix products  314 us (20%)
  local copies, waits for them, and re-layouts  69.6 us (4%)
  blocking collectives  68.8 us (4%)
  other arithmetic  32.6 us (2%)
    reduce_scatter x1, waiting for transfers between devices, shards(): lax.psum_scatter(grad_up, 'dp', scatter_dimension=0, tiled=True)  287 us
    reduce_scatter x1, waiting for transfers between devices, shards(): lax.psum_scatter(grad_down, 'dp', scatter_dimension=1, tiled=True)  286 us
    reduce_scatter x1, waiting for transfers between devices, shards(): lax.psum_scatter(grad_qkv, 'dp', scatter_dimension=0, tiled=True)  211 us
    all_gather x1, waiting for transfers between devices, shards(): lax.all_gather(w_qkv, 'dp', axis=0, tiled=True)  101 us
    dot_general x2, matrix products, one_block(): jnp.einsum('hqk,qhd->khd', grad_scores, query_block, preferred_element_ty...  47.7 us
    reduce_scatter x1, waiting for transfers between devices, shards(): lax.psum_scatter(grad_out, 'dp', scatter_dimension=1, tiled=True)  46.2 us
    dot_general x2, matrix products, one_block(): jnp.einsum('hqk,khd->qhd', grad_scores, key_rows, preferred_element_type=...  44.7 us
    psum x1, blocking collectives, shards(): lax.psum((jnp.sum(grad_ln_out * x_hat, axis=0), jnp.sum(grad_ln_out, axis...  42.2 us
  transfers between devices with their start and end apart: 12, of which 9 were waited for; matrix products, arithmetic and copies ran while one was open for 23% of the time, Pallas kernels for 0%

commit v1 on v0

--- a/solution.py
+++ b/solution.py
@@ -1,17 +1,844 @@
+import functools
+import math
+
 import jax
 import jax.numpy as jnp
 from jax import lax
+from jax.experimental import pallas as pl
+from jax.experimental.pallas import tpu as pltpu
 from jax.sharding import PartitionSpec as P
 
 HEAD_DIM = 64
 ROT = 32
-
-
 epsilon = 1e-05
 big_negative = -1e30
 
+f32 = jnp.float32
+bf16 = jnp.bfloat16
+NN = (((1,), (0,)), ((), ()))
+NT = (((1,), (1,)), ((), ()))
+TN = (((0,), (0,)), ((), ()))
+dot = functools.partial(lax.dot_general, preferred_element_type=f32)
+
+GELU_A = math.sqrt(2.0 / math.pi)
+GELU_B = 0.044715
+CHUNK = 512
+Q_BLOCK = 128
+LANES = 128
+
+
+def gelu(h):
+    return 0.5 * h * (1.0 + jnp.tanh(GELU_A * (h + GELU_B * h * h * h)))
+
+
+def gelu_slope(h):
+    t = jnp.tanh(GELU_A * (h + GELU_B * h * h * h))
+    return 0.5 * (1.0 + t) + 0.5 * h * (1.0 - t * t) * (GELU_A * (1.0 + 3.0 * GELU_B * h * h))
+
 
 def rotary_tables(row_count):
+    half_rot = ROT // 2
+    positions = jnp.arange(row_count).astype(f32)
+    freqs = 10000.0 ** (-(2.0 * jnp.arange(half_rot).astype(f32)) / ROT)
+    angles = positions[:, None] * freqs[None, :]
+    cosines, sines = jnp.cos(angles), jnp.sin(angles)
+    rest = jnp.zeros((row_count, HEAD_DIM - ROT), f32)
+    c_head = jnp.concatenate([cosines, cosines, rest + 1.0], axis=1)
+    s_head = jnp.concatenate([-sines, sines, rest], axis=1)
+    return jnp.concatenate([c_head, c_head], axis=1), jnp.concatenate([s_head, s_head], axis=1)
+
+
+def rotate(field, cosines, sines):
+    half = ROT // 2
+    lane = lax.broadcasted_iota(jnp.int32, field.shape, 1)
+    first = lax.rem(lane, HEAD_DIM) < half
+    partner = jnp.where(
+        first, pltpu.roll(field, LANES - half, 1), pltpu.roll(field, half, 1)
+    )
+    return field * cosines + partner * sines
+
+
+def block_kernel(
+    tokens, cot, gain, shift, out_bias, wq_in, wo_in, wu_in, wd_in, bq_in, bu_in, cos_t, sin_t,
+    o_out, o_gt, o_vec, o_gq, o_go, o_gu, o_gd, ry, rm, rc, rx, rl,
+    XN, G, WU, WD, WQ, WO, ACT, DH, ATT, DP, YS, FF, RING, LD, VEC, SV, SS, SR,
+    ssem, rsem, lsem,
+):
+    T, D = tokens.shape
+    R = wu_in.shape[0]
+    F = wu_in.shape[1] // 2
+    H = wo_in.shape[0] // 2
+    ROWS = 8 * T
+    LEN = 4 * T
+    half_d = D // 2
+
+    dp = lax.axis_index("dp")
+    tp = lax.axis_index("tensor")
+    hi = lax.div(dp, 4)
+    lo = lax.rem(lax.div(dp, 2), 2)
+    y = lax.rem(dp, 2)
+    x = lax.div(tp, 2)
+    c = lax.rem(tp, 2)
+
+    def device(hi_=None, lo_=None, y_=None, x_=None, c_=None):
+        a = hi if hi_ is None else hi_
+        b = lo if lo_ is None else lo_
+        d = y if y_ is None else y_
+        e = x if x_ is None else x_
+        g = c if c_ is None else c_
+        return {"dp": (a * 2 + b) * 2 + d, "tensor": e * 2 + g}
+
+    to_x = device(x_=1 - x)
+    to_c = device(c_=1 - c)
+    to_lo = device(lo_=1 - lo)
+    to_y = device(y_=1 - y)
+    to_hi = device(hi_=1 - hi)
+    to_hilo = device(hi_=1 - hi, lo_=1 - lo)
+    partners = [to_x, to_c, to_lo, to_y, to_hi, to_hilo]
+
+    def mult(v, n):
+        return pl.multiple_of(v, n)
+
+    n_copies = [0]
+    n_local = [0]
+    pending = []
+
+    class Send:
+        def __init__(self, src, dst, dev):
+            i = n_copies[0]
+            n_copies[0] += 1
+            self.d = pltpu.make_async_remote_copy(
+                src_ref=src, dst_ref=dst, send_sem=ssem.at[i], recv_sem=rsem.at[i],
+                device_id=dev, device_id_type=pl.DeviceIdType.MESH,
+            )
+            self.open = False
+
+        def start(self):
+            self.d.start()
+            self.open = True
+            pending.append(self)
+            return self
+
+        def got(self):
+            self.d.wait_recv()
+
+        def sent(self):
+            if self.open:
+                self.d.wait_send()
+                self.open = False
+
+    class Local:
+        def __init__(self, src, dst):
+            i = n_local[0]
+            n_local[0] += 1
+            self.d = pltpu.make_async_copy(src, dst, lsem.at[i])
+            self.d.start()
+            self.open = True
+
+        def wait(self):
+            if self.open:
+                self.d.wait()
+                self.open = False
+
+    def col(p, low):
+        return mult(p * 2 * R + low * R, R)
+
+    def abs_block(p, low):
+        hi_ = hi if p < 2 else 1 - hi
+        y_ = y if p % 2 == 0 else 1 - y
+        return mult(((hi_ * 2 + low) * 2 + y_) * R, R)
+
+    def row(low, xx, cc):
+        return mult((low * 4 + xx * 2 + cc) * T, T)
+
+    own_row = row(lo, x, c)
+    own_rows = pl.ds(own_row, T)
+
+    tok_loads, cot_loads = [], []
+    for p in range(4):
+        for low in range(2):
+            dst = pl.ds(p * 2 * R + low * R, R)
+            src = pl.ds(abs_block(p, low), R)
+            tok_loads.append(Local(tokens.at[:, src], RING.at[0, :, dst]))
+            cot_loads.append(Local(cot.at[:, src], G.at[own_rows, dst]))
+
+    barrier = pltpu.get_barrier_semaphore()
+    for dev in partners:
+        pl.semaphore_signal(barrier, inc=1, device_id=dev, device_id_type=pl.DeviceIdType.MESH)
+    pl.semaphore_wait(barrier, len(partners))
+
+    class Weight:
+        def __init__(self, src, land):
+            self.own = Local(src(lo), land(0, lo))
+            self.a = Send(src(1 - lo), land(0, lo), to_lo)
+            self.c = Send(src(lo), land(2, lo), to_hi)
+            self.e = Send(src(1 - lo), land(2, lo), to_hilo)
+            self.dd = Send(src(lo), land(1, lo), to_y)
+            self.f = Send(land(0, 1 - lo), land(1, 1 - lo), to_y)
+            self.g = Send(land(2, lo), land(3, lo), to_y)
+            self.h = Send(land(2, 1 - lo), land(3, 1 - lo), to_y)
+
+        def open(self):
+            self.a.start()
+            self.dd.start()
+
+        def far(self):
+            self.c.start()
+            self.e.start()
+
+        def relay_near(self):
+            self.a.got()
+            self.f.start()
+
+        def relay_far(self):
+            self.c.got()
+            self.g.start()
+            self.e.got()
+            self.h.start()
+
+        def ready(self):
+            self.own.wait()
+            for s in (self.dd, self.f, self.g, self.h):
+                s.got()
+
+    w_up = Weight(
+        lambda h: wu_in.at[:, pl.ds(mult(h * F, F), F)],
+        lambda p, low: WU.at[pl.ds(col(p, low), R), :],
+    )
+    w_q = Weight(lambda h: wq_in.at[h], lambda p, low: WQ.at[pl.ds(col(p, low), R), :])
+    w_o = Weight(
+        lambda h: wo_in.at[pl.ds(mult(h * H, H), H), :],
+        lambda p, low: WO.at[:, pl.ds(col(p, low), R)],
+    )
+    w_dn = Weight(
+        lambda h: wd_in.at[pl.ds(mult(h * F, F), F), :],
+        lambda p, low: WD.at[:, pl.ds(col(p, low), R)],
+    )
+    w_up.far()
+    w_up.open()
+
+    class Rows:
+        def __init__(self, buf):
+            def at(low, xx, cc):
+                return buf.at[pl.ds(row(low, xx, cc), T), :]
+
+            self.lo_own = Send(at(lo, x, c), at(lo, x, c), to_lo)
+            self.x_own = Send(at(lo, x, c), at(lo, x, c), to_x)
+            self.x_lo = Send(at(1 - lo, x, c), at(1 - lo, x, c), to_x)
+            self.c_own = Send(at(lo, x, c), at(lo, x, c), to_c)
+            self.c_lo = Send(at(1 - lo, x, c), at(1 - lo, x, c), to_c)
+            self.c_x = Send(at(lo, 1 - x, c), at(lo, 1 - x, c), to_c)
+            self.c_xlo = Send(at(1 - lo, 1 - x, c), at(1 - lo, 1 - x, c), to_c)
+
+        def open(self):
+            self.lo_own.start()
+            self.x_own.start()
+            self.c_own.start()
+
+        def relay_lo(self):
+            self.lo_own.got()
+            self.x_lo.start()
+            self.c_lo.start()
+
+        def relay_x(self):
+            self.x_own.got()
+            self.c_x.start()
+
+        def relay_xlo(self):
+            self.x_lo.got()
+            self.c_xlo.start()
+
+        def ready(self):
+            for s in (self.c_own, self.c_lo, self.c_x, self.c_xlo):
+                s.got()
+
+    rows_n = Rows(XN)
+    rows_g = Rows(G)
+
+    for p in range(4):
+        for low in range(2):
+            dst = pl.ds(p * 2 * R + low * R, R)
+            src = pl.ds(abs_block(p, low), R)
+            VEC[0:1, dst] = gain[:, src]
+            VEC[1:2, dst] = shift[:, src]
+            VEC[2:3, dst] = out_bias[:, src]
+    for ld in tok_loads:
+        ld.wait()
+
+    def normalise(k, sub):
+        activ = RING[k, sub, :].astype(f32)
+        average = jnp.mean(activ, axis=1, keepdims=True)
+        centered = activ - average
+        variance = jnp.mean(centered * centered, axis=1, keepdims=True)
+        inv_std = lax.rsqrt(variance + epsilon)
+        return centered * inv_std, inv_std
+
+    LN_ROWS = min(T, 64)
+
+    def ln_body(i, carry):
+        x_hat, _ = normalise(0, pl.ds(mult(i * LN_ROWS, LN_ROWS), LN_ROWS))
+        XN[pl.ds(mult(own_row + i * LN_ROWS, LN_ROWS), LN_ROWS), :] = (
+            x_hat * VEC[0:1, :] + VEC[1:2, :]
+        ).astype(bf16)
+
+    lax.fori_loop(0, T // LN_ROWS, ln_body, None)
+    rows_n.open()
+    for ld in cot_loads:
+        ld.wait()
+    rows_g.open()
+
+    SV[...] = jnp.zeros_like(SV)
+    for p in range(4):
+        for low in range(2):
+            SV[2:3, pl.ds(abs_block(p, low), R)] = jnp.sum(
+                G[own_rows, p * 2 * R + low * R : p * 2 * R + (low + 1) * R].astype(f32),
+                axis=0,
+                keepdims=True,
+            )
+
+    w_up.relay_near()
+    rows_n.relay_lo()
+    rows_n.relay_x()
+    w_up.relay_far()
+    w_q.far()
+    w_o.far()
+    w_q.open()
+    w_o.open()
+    rows_n.relay_xlo()
+    rows_g.relay_lo()
+    rows_g.relay_x()
+    w_up.ready()
+    rows_n.ready()
+
+    TILE = T
+
+    def hidden(rows):
+        return dot(XN[rows, :], WU[...], NN) + bu_in[lo]
+
+    def act_body(i, _):
+        rows = pl.ds(mult(i * TILE, TILE), TILE)
+        ACT[rows, :] = gelu(hidden(rows)).astype(bf16)
+
+    lax.fori_loop(0, ROWS // TILE, act_body, None)
+
+    w_q.relay_near()
+    w_o.relay_near()
+    rows_g.relay_xlo()
+    w_q.relay_far()
+    w_o.relay_far()
+    w_dn.far()
+    w_dn.open()
+    rows_g.ready()
+
+    def cols_of(p, q):
+        low = lo if q == 0 else 1 - lo
+        return pl.ds(col(p, low), R)
+
+    def block_dn(p, q):
+        gg = G[:, cols_of(p, q)]
+        parts = [dot(ACT[:, m * R : (m + 1) * R], gg, TN) for m in range(F // R)]
+        return [(m * R, v) for m, v in enumerate(parts)]
+
+    def block_up(p, q):
+        xx = XN[:, cols_of(p, q)]
+        return [(0, dot(xx, DH[...], TN))]
+
+    def block_at(p, q):
+        cc = cols_of(p, q)
+        return [(0, dot(XN[:, cc], DP[...], TN)), (3 * H, dot(ATT[...], G[:, cc], TN))]
+
+    class Grads:
+        def __init__(self, index, block, finals):
+            self.i = index
+            self.block = block
+            self.finals = finals
+            self.ysend = {}
+            self.msend = {}
+            for k, (p, q) in enumerate(((3, 1), (3, 0), (1, 1), (1, 0))):
+                self.ysend[p, q] = Send(YS.at[index, k], ry.at[index, k], to_y)
+            for q in (1, 0):
+                self.msend[q] = Send(YS.at[index, 1 - q], rm.at[index, 1 - q], to_hi)
+
+        def slot(self, p, q):
+            return (0 if p >= 2 else 2) + (1 - q)
+
+        def near(self, p):
+            for q in (1, 0):
+                k = self.slot(p, q)
+                for off, v in self.block(p, q):
+                    YS[self.i, k, :, off : off + v.shape[1]] = v.astype(bf16)
+                self.ysend[p, q].start()
+
+        def far(self, q):
+            k = self.slot(2, q)
+            self.ysend[3, q].got()
+            load = Local(ry.at[self.i, k], LD.at[0, :, 0:F])
+            vals = self.block(2, q)
+            self.ysend[3, q].sent()
+            load.wait()
+            for off, v in vals:
+                n = v.shape[1]
+                YS[self.i, k, :, off : off + n] = (
+                    v + LD[0, :, off : off + n].astype(f32)
+                ).astype(bf16)
+            self.msend[q].start()
+
+        def last(self, q):
+            k = self.slot(0, q)
+            settle((q,))
+            self.ysend[1, q].got()
+            load = Local(ry.at[self.i, k], LD.at[0, :, 0:F])
+            vals = self.block(0, q)
+            load.wait()
+            for off, v in vals:
+                n = v.shape[1]
+                FF[q, :, off : off + n] = v + LD[0, :, off : off + n].astype(f32)
+            self.msend[q].got()
+            load = Local(rm.at[self.i, 1 - q], LD.at[1, :, 0:F])
+            load.wait()
+            FF[q, :, :] += LD[1, :, 0:F].astype(f32)
+            for src, dst in self.finals(FF.at[q], lo):
+                if q == 1:
+                    final_out[q].append(Send(src, dst, to_lo).start())
+                    final_in.append(final_out[q][-1])
+                else:
+                    final_out[q].append(Local(src, dst))
+
+    final_out = {0: [], 1: []}
+    final_in = []
+
+    def settle(which=(0, 1)):
+        for q in which:
+            for s in final_out[q]:
+                if isinstance(s, Send):
+                    s.sent()
+                else:
+                    s.wait()
+            final_out[q] = []
+
+    gr_dn = Grads(
+        0, block_dn,
+        lambda src, h: [
+            (src.at[:, pl.ds(m * R, R)], o_gd.at[pl.ds(mult(h * F + m * R, R), R), :])
+            for m in range(F // R)
+        ],
+    )
+    gr_at = Grads(
+        1, block_at,
+        lambda src, h: [
+            (src.at[:, pl.ds(0, 3 * H)], o_gq.at[h]),
+            (src.at[:, pl.ds(3 * H, R)], o_go.at[pl.ds(mult(h * H, H), H), :]),
+        ],
+    )
+    gr_up = Grads(2, block_up, lambda src, h: [(src, o_gu.at[:, pl.ds(mult(h * F, F), F)])])
+
+    gr_dn.near(3)
+    gr_dn.near(1)
+    for w in (w_q, w_o):
+        w.ready()
+
+    Q, K, V, DA = (0, 0), (0, 4 * H), (1, 0), (1, 4 * H)
+
+    def head_rows(which, start, size, cc):
+        slot, base = which
+        got = []
+        at = start
+        while at < start + size:
+            stop = min((at // T + 1) * T, start + size)
+            cols = pl.ds(mult(base + at // T * H + cc, LANES), LANES)
+            got.append(RING[slot, at % T : at % T + stop - at, cols])
+            at = stop
+        return got[0] if len(got) == 1 else jnp.concatenate(got, axis=0)
+
+    def project(s):
+        def body(i, _):
+            pos = pl.ds(mult(i * T, T), T)
+            rows = pl.ds(mult((s * 4 + i) * T, T), T)
+            pr = dot(XN[rows, :], WQ[...], NN) + bq_in[lo]
+            cs, sn = cos_t[pos, :], sin_t[pos, :]
+
+            def put(which, a, v):
+                RING[which[0], :, pl.ds(mult(which[1] + i * H + a, LANES), LANES)] = v.astype(bf16)
+
+            d_att = dot(G[rows, :], WO[...], NT)
+            for h in range(H // LANES):
+                a = h * LANES
+                put(Q, a, rotate(pr[:, a : a + LANES], cs, sn))
+                put(K, a, rotate(pr[:, H + a : H + a + LANES], cs, sn))
+                put(V, a, pr[:, 2 * H + a : 2 * H + a + LANES])
+                put(DA, a, d_att[:, a : a + LANES])
+
+        lax.fori_loop(0, 4, body, None)
+
+    def attend(s):
+        first = lax.broadcasted_iota(jnp.int32, (Q_BLOCK, LANES), 1) < HEAD_DIM
+        scaling = HEAD_DIM**-0.5
+
+        def split(v):
+            zero = jnp.zeros_like(v)
+            return jnp.concatenate([jnp.where(first, v, zero), jnp.where(first, zero, v)], axis=0)
+
+        def join(v):
+            return jnp.where(first, v[:Q_BLOCK], v[Q_BLOCK:])
+
+        def piece(j):
+            at = j * Q_BLOCK
+            return pl.ds(at % T, Q_BLOCK), pl.ds(at // T * LANES, LANES)
+
+        def pair(hp, _):
+            cc = hp * LANES
+            out_cols = pl.ds(mult(cc, LANES), LANES)
+            for i in range(LEN // Q_BLOCK):
+                rr = pl.ds(i * Q_BLOCK, Q_BLOCK)
+                out_rows = pl.ds(s * LEN + i * Q_BLOCK, Q_BLOCK)
+                n = (i + 1) * Q_BLOCK
+                old = n - Q_BLOCK
+                qm = split(head_rows(Q, old, Q_BLOCK, cc))
+                dm = split(head_rows(DA, old, Q_BLOCK, cc))
+                kk = head_rows(K, 0, n, cc)
+                vv = head_rows(V, 0, n, cc)
+                st = dot(kk, qm * jnp.asarray(scaling, bf16), NT)
+                kpos = lax.broadcasted_iota(jnp.int32, (Q_BLOCK, 2 * Q_BLOCK), 0)
+                qpos = lax.broadcasted_iota(jnp.int32, (Q_BLOCK, 2 * Q_BLOCK), 1)
+                qpos = jnp.where(qpos < Q_BLOCK, qpos, qpos - Q_BLOCK)
+                diagonal = jnp.where(kpos <= qpos, st[old:], big_negative)
+                st = diagonal if i == 0 else jnp.concatenate([st[:old], diagonal], axis=0)
+                ex = jnp.exp(st - jnp.max(st, axis=0, keepdims=True))
+                prob = ex * (1.0 / jnp.sum(ex, axis=0, keepdims=True))
+                pb = prob.astype(bf16)
+                ATT[out_rows, out_cols] = join(dot(pb, vv, TN)).astype(bf16)
+                dv = dot(pb, dm, NN)
+                dprob = dot(vv, dm, NT)
+                centre = jnp.sum(dprob * prob, axis=0, keepdims=True)
+                ds = (prob * (dprob - centre) * scaling).astype(bf16)
+                dq = join(dot(ds, kk, TN))
+                DP[out_rows, out_cols] = rotate(dq, cos_t[rr, :], -sin_t[rr, :]).astype(bf16)
+                dk = dot(ds, qm, NN)
+                for j in range(i + 1):
+                    pr, pc = piece(j)
+                    part = slice(j * Q_BLOCK, (j + 1) * Q_BLOCK)
+                    if j < i:
+                        FF[0, pr, pc] += dk[part]
+                        FF[1, pr, pc] += dv[part]
+                    else:
+                        FF[0, pr, pc] = dk[part]
+                        FF[1, pr, pc] = dv[part]
+            for j in range(LEN // Q_BLOCK):
+                pr, pc = piece(j)
+                rr = pl.ds(j * Q_BLOCK, Q_BLOCK)
+                out_rows = pl.ds(s * LEN + j * Q_BLOCK, Q_BLOCK)
+                DP[out_rows, pl.ds(mult(H + cc, LANES), LANES)] = rotate(
+                    FF[0, pr, pc], cos_t[rr, :], -sin_t[rr, :]
+                ).astype(bf16)
+                DP[out_rows, pl.ds(mult(2 * H + cc, LANES), LANES)] = FF[1, pr, pc].astype(bf16)
+
+        lax.fori_loop(0, H // LANES, pair, None)
+
+    project(0)
+    attend(0)
+    w_dn.relay_near()
+    project(1)
+    w_dn.relay_far()
+    gr_dn.far(1)
+    gr_dn.far(0)
+    attend(1)
+
+    gr_at.near(3)
+    gr_at.near(1)
+
+    def rows_out(rr, cc):
+        return dot(ACT[rr, :], WD[:, cc], NN) + dot(ATT[rr, :], WO[:, cc], NN)
+
+    def rows_dn(rr, cc):
+        return dot(DH[rr, :], WU[cc, :], NT) + dot(DP[rr, :], WQ[cc, :], NT)
+
+    ring_use = {0: None, 1: None, 2: None}
+    ring_next = [0]
+
+    def ring_slot():
+        i = ring_next[0]
+        ring_next[0] = (i + 1) % 3
+        if ring_use[i] is not None:
+            ring_use[i].sent()
+            ring_use[i] = None
+        return i
+
+    class Owner:
+        def __init__(self, index, partial):
+            self.i = index
+            self.partial = partial
+            self.cs, self.xs = {}, {}
+
+        def chunks(self, low, xx, cc, loads, store):
+            rr = pl.ds(row(low, xx, cc), T)
+            for ld in loads:
+                ld.wait()
+
+            def body(j, _):
+                cols = pl.ds(mult(j * CHUNK, CHUNK), CHUNK)
+                v = self.partial(rr, cols)
+                for k in range(len(loads)):
+                    v = v + LD[k, :, cols].astype(f32)
+                store(j, cols, v)
+
+            lax.fori_loop(0, D // CHUNK, body, None)
+
+        def put(self, low, xx, cc, srcs, dst, dev):
+            loads = [Local(src, LD.at[k]) for k, src in enumerate(srcs)]
+            k = ring_slot()
+
+            def store(j, cols, v):
+                RING[k, :, cols] = v.astype(bf16)
+
+            self.chunks(low, xx, cc, loads, store)
+            s = Send(RING.at[k], dst, dev).start()
+            ring_use[k] = s
+            return s
+
+        def core(self):
+            for dlo, dx in ((1, 1), (0, 1), (1, 0), (0, 0)):
+                low = lo if dlo == 0 else 1 - lo
+                xx = x if dx == 0 else 1 - x
+                self.cs[dlo, dx] = self.put(
+                    low, xx, 1 - c, [], rc.at[self.i, 2 * dlo + dx], to_c
+                )
+
+        def cross(self):
+            for dlo in (1, 0):
+                low = lo if dlo == 0 else 1 - lo
+                self.cs[dlo, 1].got()
+                self.xs[dlo] = self.put(
+                    low, 1 - x, c, [rc.at[self.i, 2 * dlo + 1]], rx.at[self.i, dlo], to_x
+                )
+
+        def level(self):
+            self.cs[1, 0].got()
+            self.xs[1].got()
+            self.ls = self.put(
+                1 - lo, x, c, [rc.at[self.i, 2], rx.at[self.i, 1]], rl.at[self.i], to_lo
+            )
+
+        def own(self):
+            self.cs[0, 0].got()
+            self.xs[0].got()
+            loads = [Local(rc.at[self.i, 0], LD.at[0]), Local(rx.at[self.i, 0], LD.at[1])]
+
+            def store(j, cols, v):
+                FF[lax.div(j, D // CHUNK // 2), :, pl.ds(mult(lax.rem(j, D // CHUNK // 2) * CHUNK, CHUNK), CHUNK)] = v
+
+            self.chunks(lo, x, c, loads, store)
+            self.ls.got()
+            Local(rl.at[self.i], LD.at[0]).wait()
+
+    def own_sub(sub):
+        return jnp.concatenate([FF[0, sub, :], FF[1, sub, :]], axis=1) + LD[0, sub, :].astype(f32)
+
+    own_out = Owner(0, rows_out)
+    own_dn = Owner(1, rows_dn)
+
+    w_dn.ready()
+    own_out.core()
+
+    VEC[3:4, 0:F] = jnp.zeros((1, F), f32)
+
+    def dh_body(i, _):
+        rows = pl.ds(mult(i * TILE, TILE), TILE)
+        d_act = dot(G[rows, :], WD[...], NT)
+        dh = (d_act * gelu_slope(hidden(rows))).astype(bf16)
+        DH[rows, :] = dh
+        VEC[3:4, 0:F] += jnp.sum(dh.astype(f32), axis=0, keepdims=True)
+
+    lax.fori_loop(0, ROWS // TILE // 2, dh_body, None)
+    own_out.cross()
+    lax.fori_loop(ROWS // TILE // 2, ROWS // TILE, dh_body, None)
+
+    own_dn.core()
+    gr_up.near(3)
+    gr_up.near(1)
+    gr_at.far(1)
+    gr_at.far(0)
+    own_dn.cross()
+    gr_dn.last(1)
+    gr_dn.last(0)
+    gr_up.far(1)
+    gr_up.far(0)
+
+    SV[3:4, pl.ds(mult(lo * F, F), F)] = VEC[3:4, 0:F]
+    VEC[4:5, 0 : 3 * H] = jnp.zeros((1, 3 * H), f32)
+
+    def dp_body(i, _):
+        VEC[4:5, 0 : 3 * H] += jnp.sum(
+            DP[pl.ds(mult(i * T, T), T), :].astype(f32), axis=0, keepdims=True
+        )
+
+    lax.fori_loop(0, ROWS // T, dp_body, None)
+    SV[4:5, pl.ds(mult(lo * 3 * H, LANES), 3 * H)] = VEC[4:5, 0 : 3 * H]
+
+    own_out.level()
+    settle()
+
+    def load_tokens():
+        k = ring_slot()
+        return k, [
+            Local(
+                tokens.at[:, pl.ds(abs_block(p, low), R)],
+                RING.at[k, :, pl.ds(p * 2 * R + low * R, R)],
+            )
+            for p in range(4)
+            for low in range(2)
+        ]
+
+    k_tok, tok_ld = load_tokens()
+    own_out.own()
+    for ld in tok_ld:
+        ld.wait()
+    k_out = ring_slot()
+
+    def out_body(i, _):
+        sub = pl.ds(mult(i * LN_ROWS, LN_ROWS), LN_ROWS)
+        RING[k_out, sub, :] = (
+            RING[k_tok, sub, :].astype(f32) + own_sub(sub) + VEC[2:3, :]
+        ).astype(bf16)
+
+    lax.fori_loop(0, T // LN_ROWS, out_body, None)
+    out_st = [
+        Local(
+            RING.at[k_out, :, pl.ds(p * 2 * R + low * R, R)],
+            o_out.at[:, pl.ds(abs_block(p, low), R)],
+        )
+        for p in range(4)
+        for low in range(2)
+    ]
+    for st in out_st:
+        st.wait()
+
+    gr_at.last(1)
+    own_dn.level()
+    gr_at.last(0)
+    settle()
+
+    k_x, tok_ld = load_tokens()
+    own_dn.own()
+    for ld in tok_ld:
+        ld.wait()
+    VEC[4:6, :] = jnp.zeros((2, D), f32)
+
+    def gt_body(i, _):
+        sub = pl.ds(mult(i * LN_ROWS, LN_ROWS), LN_ROWS)
+        x_hat, inv_std = normalise(k_x, sub)
+        dn = own_sub(sub)
+        VEC[4:5, :] += jnp.sum(dn * x_hat, axis=0, keepdims=True)
+        VEC[5:6, :] += jnp.sum(dn, axis=0, keepdims=True)
+        scaled = dn * VEC[0:1, :]
+        gt = (
+            inv_std
+            * (
+                scaled
+                - jnp.mean(scaled, axis=1, keepdims=True)
+                - x_hat * jnp.mean(scaled * x_hat, axis=1, keepdims=True)
+            )
+            + G[pl.ds(mult(own_row + i * LN_ROWS, LN_ROWS), LN_ROWS), :].astype(f32)
+        )
+        FF[0, sub, :] = gt[:, :half_d]
+        FF[1, sub, :] = gt[:, half_d:]
+
+    lax.fori_loop(0, T // LN_ROWS, gt_body, None)
+    gt_st = []
+    for p in range(4):
+        for low in range(2):
+            off = (p % 2) * 2 * R + low * R
+            dst = pl.ds(abs_block(p, low), R)
+            src = slice(p * 2 * R + low * R, p * 2 * R + (low + 1) * R)
+            gt_st.append(Local(FF.at[p // 2, :, pl.ds(off, R)], o_gt.at[:, dst]))
+            SV[0:2, dst] = VEC[4:6, src]
+
+    for k, dev in enumerate((to_y, to_hi, to_lo, to_x, to_c)):
+        SS[k, :, :] = SV[...]
+        s = Send(SS.at[k], SR.at[k], dev).start()
+        s.got()
+        if k < 3:
+            SV[...] += SR[k]
+        else:
+            SV[0:3, :] += SR[k, 0:3, :]
+    o_vec[...] = SV[...]
+
+    for st in gt_st:
+        st.wait()
+    gr_up.last(1)
+    gr_up.last(0)
+    settle()
+    for s in final_in:
+        s.got()
+    for s in pending:
+        s.sent()
+    assert n_copies[0] <= ssem.shape[0], n_copies
+    assert n_local[0] <= lsem.shape[0], n_local
+
+
+def fast_shards(tokens, ln_gain, ln_bias, w_qkv, b_qkv, w_out, w_up, b_up, w_down, out_bias, cot):
+    T, D = tokens.shape
+    R, F = w_up.shape[0], w_up.shape[1] // 2
+    H = w_out.shape[0] // 2
+    cos_t, sin_t = rotary_tables(4 * T)
+    wq = w_qkv.reshape(R, 3, 2, H).transpose(2, 0, 1, 3).reshape(2, R, 3 * H)
+    bq = b_qkv.reshape(3, 2, H).transpose(1, 0, 2).reshape(2, 1, 3 * H)
+    bu = b_up.reshape(2, 1, F)
+    S = jax.ShapeDtypeStruct
+    hbm = pl.BlockSpec(memory_space=pl.ANY)
+    vm = pl.BlockSpec(memory_space=pltpu.VMEM)
+    outs = pl.pallas_call(
+        block_kernel,
+        out_shape=(
+            S((T, D), bf16), S((T, D), f32), S((8, D), f32),
+            S((2, R, 3 * H), f32), S((2 * H, R), f32), S((R, 2 * F), f32), S((2 * F, R), f32),
+            S((3, 4, R, F), bf16), S((3, 2, R, F), bf16),
+            S((2, 4, T, D), bf16), S((2, 2, T, D), bf16), S((2, T, D), bf16),
+        ),
+        in_specs=[hbm, hbm, vm, vm, vm, hbm, hbm, hbm, hbm, vm, vm, vm, vm],
+        out_specs=(hbm, hbm, vm) + (hbm,) * 9,
+        scratch_shapes=[
+            pltpu.VMEM((8 * T, D), bf16),
+            pltpu.VMEM((8 * T, D), bf16),
+            pltpu.VMEM((D, F), bf16),
+            pltpu.VMEM((F, D), bf16),
+            pltpu.VMEM((D, 3 * H), bf16),
+            pltpu.VMEM((H, D), bf16),
+            pltpu.VMEM((8 * T, F), bf16),
+            pltpu.VMEM((8 * T, F), bf16),
+            pltpu.VMEM((8 * T, H), bf16),
+            pltpu.VMEM((8 * T, 3 * H), bf16),
+            pltpu.VMEM((3, 4, R, F), bf16),
+            pltpu.VMEM((2, R, F), f32),
+            pltpu.VMEM((3, T, D), bf16),
+            pltpu.VMEM((2, T, D), bf16),
+            pltpu.VMEM((8, D), f32),
+            pltpu.VMEM((8, D), f32),
+            pltpu.VMEM((5, 8, D), f32),
+            pltpu.VMEM((5, 8, D), f32),
+            pltpu.SemaphoreType.DMA((90,)),
+            pltpu.SemaphoreType.DMA((90,)),
+            pltpu.SemaphoreType.DMA((110,)),
+        ],
+        compiler_params=pltpu.CompilerParams(
+            collective_id=0, has_side_effects=True, vmem_limit_bytes=VMEM_LIMIT
+        ),
+        name="parallel_block",
+    )(
+        tokens, cot, ln_gain.reshape(1, D), ln_bias.reshape(1, D), out_bias.reshape(1, D),
+        wq, w_out, w_up, w_down, bq, bu, cos_t, sin_t,
+    )
+    o_out, o_gt, o_vec, o_gq, o_go, o_gu, o_gd = outs[:7]
+    g_qkv = o_gq.reshape(2, R, 3, H).transpose(1, 2, 0, 3).reshape(R, 3, 2 * H)
+    g_bq = o_vec[4, : 6 * H].reshape(2, 3, H).transpose(1, 0, 2).reshape(3, 2 * H)
+    return (
+        o_out, o_gt, o_vec[0], o_vec[1], g_qkv, g_bq, o_go, o_gu, o_vec[3, : 2 * F], o_gd, o_vec[2],
+    )
+
+
+VMEM_LIMIT = 64 << 20
+
+
+def plain_tables(row_count):
     half_rot = ROT // 2
     positions = jnp.arange(row_count).astype(jnp.float32)
     freqs = 10000.0 ** (-(2.0 * jnp.arange(half_rot).astype(jnp.float32)) / ROT)
@@ -19,7 +846,7 @@
     return (jnp.cos(angles)[:, None, :], jnp.sin(angles)[:, None, :])
 
 
-def rotate(field, cosines, sines):
+def plain_rotate(field, cosines, sines):
     half_rot = ROT // 2
     first = field[..., :half_rot]
     second = field[..., half_rot:ROT]
@@ -101,7 +928,7 @@
     return (grad_queries.reshape(row_count, heads_here, head_size), grad_keys, grad_values)
 
 
-def shards(tokens, ln_gain, ln_bias, w_qkv, b_qkv, w_out, w_up, b_up, w_down, out_bias, cotangent):
+def plain_shards(tokens, ln_gain, ln_bias, w_qkv, b_qkv, w_out, w_up, b_up, w_down, out_bias, cotangent):
     activ = tokens.astype(jnp.float32)
     average = jnp.mean(activ, axis=1, keepdims=True)
     centered = activ - average
@@ -125,9 +952,9 @@
     project = (
         jnp.einsum("td,dcf->tcf", normed, qkv_full, preferred_element_type=jnp.float32) + b_qkv
     )
-    cosines, sines = rotary_tables(row_count)
-    queries = rotate(project[:, 0].reshape(head_shape), cosines, sines).astype(jnp.bfloat16)
-    key_rows = rotate(project[:, 1].reshape(head_shape), cosines, sines).astype(jnp.bfloat16)
+    cosines, sines = plain_tables(row_count)
+    queries = plain_rotate(project[:, 0].reshape(head_shape), cosines, sines).astype(jnp.bfloat16)
+    key_rows = plain_rotate(project[:, 1].reshape(head_shape), cosines, sines).astype(jnp.bfloat16)
     value_rows = project[:, 2].reshape(head_shape).astype(jnp.bfloat16)
     attended, logsum = attend_forward(queries, key_rows, value_rows, block_len)
     attended = attended.astype(jnp.bfloat16)
@@ -154,8 +981,8 @@
     grad_queries, grad_keys, grad_values = attend_backward(
         queries, key_rows, value_rows, grad_att.reshape(head_shape), logsum, block_len
     )
-    grad_q_pre = rotate(grad_queries, cosines, -sines).reshape(row_count, local_width)
-    grad_k_pre = rotate(grad_keys, cosines, -sines).reshape(row_count, local_width)
+    grad_q_pre = plain_rotate(grad_queries, cosines, -sines).reshape(row_count, local_width)
+    grad_k_pre = plain_rotate(grad_keys, cosines, -sines).reshape(row_count, local_width)
     grad_project = jnp.stack(
         [grad_q_pre, grad_k_pre, grad_values.reshape(row_count, local_width)], axis=1
     ).astype(jnp.bfloat16)
@@ -219,22 +1046,24 @@
         P(),
         P(("dp", "tensor"), None),
     )
+    results = (
+        P(("dp", "tensor"), None),
+        P(("dp", "tensor"), None),
+        P(),
+        P(),
+        P("dp", None, "tensor"),
+        P(None, "tensor"),
+        P("tensor", "dp"),
+        P("dp", "tensor"),
+        P("tensor"),
+        P("tensor", "dp"),
+        P(),
+    )
+    one_kernel = mesh.shape["dp"] == 8 and mesh.shape["tensor"] == 4
     return jax.shard_map(
-        shards,
+        fast_shards if one_kernel else plain_shards,
         mesh=mesh,
         in_specs=placed,
-        out_specs=(
-            P(("dp", "tensor"), None),
-            P(("dp", "tensor"), None),
-            P(),
-            P(),
-            P("dp", None, "tensor"),
-            P(None, "tensor"),
-            P("tensor", "dp"),
-            P("dp", "tensor"),
-            P("tensor"),
-            P("tensor", "dp"),
-            P(),
-        ),
+        out_specs=results,
         check_vma=False,
     )

time: 1590 us -> 552 us (0.35)
  waiting for transfers between devices: 1080 us -> 0 us
  Pallas kernels: 0 us -> 515 us
  matrix products: 314 us -> 0 us
  blocking collectives: 68.8 us -> 0 us
  local copies, waits for them, and re-layouts: 69.6 us -> 22.6 us
  other arithmetic: 32.6 us -> 1.91 us
    reduce_scatter x6 -> x0, waiting for transfers between devices: 867 us -> none  [the longest x1 287 us: shards(): lax.psum_scatter(grad_up, 'dp', scatter_dimension=0, tiled=True)]
    pallas_call x0 -> x1, Pallas kernels: none -> 515 us  [fast_shards(): pl.pallas_call(block_kernel, out_shape=(S((T, D), bf16), S((T, D), f32),...]
    dot_general x26 -> x0, matrix products: 314 us -> none  [the longest x2 47.7 us: one_block(): jnp.einsum('hqk,qhd->khd', grad_scores, query_block, preferred_element_ty...]
    all_gather x6 -> x0, waiting for transfers between devices: 206 us -> none  [the longest x1 101 us: shards(): lax.all_gather(w_qkv, 'dp', axis=0, tiled=True)]
    psum x2 -> x0, blocking collectives: 68.8 us -> none  [the longest x1 42.2 us: shards(): lax.psum((jnp.sum(grad_ln_out * x_hat, axis=0), jnp.sum(grad_ln_out, axis...]
    dynamic_update_slice x4 -> x0, local copies, waits for them, and re-layouts: 41.4 us -> none  [attend_forward(): attended, logsum = lax.map(one_block, (query_blocks, jnp.arange(n_blocks)))]
    reduce_sum x7 -> x0, other arithmetic: 21.6 us -> none  [the longest x2 8.49 us: one_block(): totals = jnp.sum(exponent, axis=2, keepdims=True)]
  transfers between devices with their start and end apart: 12 -> 0, of which waited for: 9 -> 0; matrix products, arithmetic and copies ran while one was open for 23% -> 0% of each run, Pallas kernels for 0% -> 0%
where the time goes in v1:
time: 552 us; the launch traced here: 541 us
  Pallas kernels  515 us (93%)
  local copies, waits for them, and re-layouts  22.6 us (4%)
    pallas_call x1, Pallas kernels, fast_shards(): pl.pallas_call(block_kernel, out_shape=(S((T, D), bf16), S((T, D), f32),...  515 us
    unnamed x17, local copies, waits for them, and re-layouts  11.4 us

profile of v1, /device:TPU:27, one launch (start us, length us, event | category | flops | bytes accessed | tf_op | source)
XLA Modules:
  0.0 540.8 jit_solution(6308842281409890826)
XLA Ops:
  0.7 1.3 reshape.78.bq_in
  2.0 1.4 copy.38
  3.4 0.1 copy.39
  3.4 1.2 copy.42.wq_in
  4.6 1.9 multiply_sine_fusion
  6.5 1.7 concatenate.10.cos_t
  8.3 1.7 concatenate.11.sin_t
  10.1 515.1 %parallel_block.1 = (bf16[256,2048]{1,0:T(8,128)(2,1)}, f32[256,2048]{1,0:T(8,128)}, f32[8,2048]{1,0:T(8,128)}, f32[2,256,768]{2,1,0:T(8,128)}, f32[512,256]{1,0...) custom-call(bf16[256,2048]{1,0:T(8,128)(2,1)} %tokens.1, ...), custom_call_target="tpu_custom_call" | custom-call | tf_op jit(solution)/shard_map/parallel_block/pallas_call | solution.py:789
  525.2 0.8 slice_reduce_fusion
  526.0 1.7 fusion.1
  527.7 0.6 reshape_squeeze.3
  528.3 1.9 copy.44
  530.2 0.2 copy.45
  530.4 0.0 copy-start.3
  530.4 1.6 copy.46
  532.0 0.0 copy-done.3
  532.0 0.0 copy-start.2
  532.0 1.0 copy.52
  533.0 1.0 copy-done.2
  534.0 0.0 copy-start.4
  534.0 0.0 copy-start.1
  534.0 1.3 copy.53
  535.3 0.1 copy-done.4
  535.3 0.8 copy.54
  536.1 0.5 copy-done.1
  536.7 0.0 copy-start
  536.7 1.3 copy.55
  538.0 1.0 copy-done
  539.0 1.3 copy.56
  (4 shorter events, 0.1 us)
Async XLA Ops:
  530.4 1.6 copy-start.3
  532.0 2.0 copy-start.2
  534.0 1.4 copy-start.4
  534.0 2.7 copy-start.1
  536.7 2.3 copy-start
